TPU v7x, 32 devices: a whole 2x2x4 slice. The times are simulated.
32 devices in a mesh: ta: 16 (over z, x, core), pa: 2 (over y).
Axes of the slice: x: 2, y: 2, z: 4, core: 2. Of those that a mesh axis runs over, the one named last changes fastest.
Arguments:
- occupied_orbitals: bfloat16 [4096, 512], P('pa'), may hold values from -3 to 3
- virtual_orbitals: bfloat16 [4096, 1536], P('pa'), may hold values from -2.5 to 2.5
- occupied_gaps: float32 [512], replicated, may hold values from 0.05 to 2
- virtual_gaps: float32 [1536], replicated, may hold values from 0.05 to 2
- tile_columns: int32 [32, 8], replicated, may hold values from 0 to 31, as said below
- probe_vectors: bfloat16 [32, 4096], P(None, 'ta'), may hold values from -0.1875 to 0.1875
Outputs:
- response: float32 [16, 32, 4096], P('ta', None, 'pa')
Inputs may be any that keep to these rules, and one draw needn't show every extreme that they name: `tile_columns`: each row block lists 8 different column blocks, and every column block is listed by some row block.
All inputs are finite; a program needn't handle non-finite values.
Results may differ from a plain program's by a relative error of at most 0.00083.
Values may be sent and summed in bfloat16 or wider, within the bound.
No kernel may reach another device: no remote copies, remote signals or barrier semaphores. Data moves between devices by JAX's collectives and lax.ppermute only.
A program may use at most 128 MiB of HBM per device.

v0:
```python
import functools

import jax
import jax.numpy as jnp
from jax import lax
from jax.experimental import pallas as pl
from jax.experimental.pallas import tpu as pltpu
from jax.sharding import PartitionSpec as P

BLK = 128
NT = 32
NVEC = 32
FREQS = 4
LARGE = pltpu.CompilerParams(vmem_limit_bytes=52 * 2**20)
SMALL = pltpu.CompilerParams(vmem_limit_bytes=52 * 2**20)
NT_DIMS = (((1,), (1,)), ((), ()))
ANY = pl.BlockSpec(memory_space=pl.ANY)
SMEM = pl.BlockSpec(memory_space=pltpu.SMEM)
VMEM = pl.BlockSpec(memory_space=pltpu.VMEM)


def quadrature_grids(count_times, count_freqs):
    low_time = jnp.log(jnp.float32(0.05))
    high_time = jnp.log(jnp.float32(8.0))
    time_place = (jnp.arange(count_times, dtype=jnp.float32) + 0.5) / count_times
    times_grid = jnp.exp(low_time + (high_time - low_time) * time_place)
    weights_grid = times_grid * (high_time - low_time) / count_times
    low_freq = jnp.log(jnp.float32(0.05))
    high_freq = jnp.log(jnp.float32(20.0))
    freq_place = (jnp.arange(count_freqs, dtype=jnp.float32) + 0.5) / count_freqs
    freqs_grid = jnp.exp(low_freq + (high_freq - low_freq) * freq_place)
    cosine_table = 2.0 * weights_grid[None, :] * jnp.cos(freqs_grid[:, None] * times_grid[None, :])
    return (times_grid, cosine_table)


class Plan:
    def __init__(self, panels, tiles, blocks):
        self.panels = panels
        self.tiles = tiles
        self.blocks = blocks
        self.cols = panels
        self.order = panels + panels * tiles
        self.size = self.order + blocks


def pack_kernel(group, occ, virt, sent, sems):
    slot = lax.div(lax.axis_index("ta"), jnp.int32(group))
    virt_count = virt.shape[1]
    place = pl.ds(pl.multiple_of(slot * BLK, BLK), BLK)
    copies = (
        pltpu.make_async_copy(virt.at[place, :], sent.at[:, pl.ds(0, virt_count)], sems.at[0]),
        pltpu.make_async_copy(
            occ.at[place, :], sent.at[:, pl.ds(virt_count, occ.shape[1])], sems.at[1]
        ),
    )
    for copy in copies:
        copy.start()
    for copy in copies:
        copy.wait()


def plan_kernel(
    plan, group, tiles_hbm, probe_hbm, after, out, spread,
    listed, probe, keys, places, ranked, sems,
):
    panels, tiles, blocks = plan.panels, plan.tiles, plan.blocks
    here = lax.axis_index("pa")
    slot = lax.div(lax.axis_index("ta"), jnp.int32(group))
    copy_tiles = pltpu.make_async_copy(tiles_hbm, listed, sems.at[0])
    copy_probe = pltpu.make_async_copy(probe_hbm, probe, sems.at[1])
    copy_tiles.start()
    copy_probe.start()
    copy_tiles.wait()

    low = here * blocks

    def inside(row, k):
        column = listed[row, k]
        return ((column >= low) & (column < low + blocks)).astype(jnp.int32)

    def count(row):
        total = jnp.int32(0)
        for k in range(tiles):
            total += inside(row, k)
        return total

    most = max(tiles, tiles * (panels - 1))
    for kind in range(2):
        for value in range(most + 2):
            places[kind, value] = 0

    def one_count(s, carry):
        total = jnp.int32(0)
        for offset in range(1, panels):
            total += count(lax.rem(here + offset, panels) * blocks + s)
        for kind, value in enumerate((count(low + s), most - total)):
            keys[kind, s] = value
            places[kind, value + 1] = places[kind, value + 1] + 1
        return carry

    lax.fori_loop(0, blocks, one_count, 0)
    for kind in range(2):
        first = jnp.int32(0)
        for value in range(1, most + 2):
            first += places[kind, value]
            places[kind, value] = first

    def one_place(s, carry):
        for kind in range(2):
            value = keys[kind, s]
            rank = places[kind, value]
            places[kind, value] = rank + 1
            ranked[kind, rank] = s
        return carry

    lax.fori_loop(0, blocks, one_place, 0)
    for rank in range(blocks):
        out[plan.order + ranked[1, rank]] = ranked[0, rank]

    for which in range(panels):
        if which < panels - 1:
            row = lax.rem(here + which + 1, panels) * blocks + slot
        else:
            row = low + out[plan.order + slot]
        total = jnp.int32(0)
        for k in range(tiles):
            out[plan.cols + which * tiles + total] = listed[row, k] - low
            total += inside(row, k)
        out[which] = total

    copy_probe.wait()
    width = spread.shape[3]
    for piece in range(spread.shape[1]):
        value = probe[:, piece * width : (piece + 1) * width]
        for target in range(spread.shape[0]):
            spread[target, piece] = value


def scale_part(first_time, times, gaps_occ, gaps_virt, row_occ, row_virt, scaled, unrolled):
    def one_time(u, carry):
        place = pl.ds(u * BLK if unrolled else pl.multiple_of(u * BLK, BLK), BLK)
        minus_time = -times[first_time + u]
        for gaps, row, target in zip((gaps_occ, gaps_virt), (row_occ, row_virt), scaled):
            weights = jnp.exp(minus_time * gaps[...].reshape(1, -1))
            target[place, :] = (row[...].astype(jnp.float32) * weights).astype(jnp.bfloat16)
        return carry

    count = scaled[0].shape[0] // BLK
    if unrolled:
        for u in range(count):
            one_time(u, 0)
    else:
        lax.fori_loop(0, count, one_time, 0)


def starts_of(scaled):
    starts = [0]
    for part in scaled:
        starts.append(starts[-1] + part[0].shape[0])
    return starts


def loaded_tiles(count):
    return jnp.where(count == 1, 2, count)


def tile_copies(plan, table, which, tile, occ, virt, cols_occ, cols_virt, sems):
    last = jnp.maximum(table[which] - 1, 0)
    column = table[plan.cols + which * plan.tiles + jnp.minimum(tile, last)]
    source = pl.ds(pl.multiple_of(column * BLK, BLK), BLK)
    target = pl.ds(pl.multiple_of(tile * BLK, BLK), BLK)
    return (
        pltpu.make_async_copy(occ.at[source, :], cols_occ.at[target, :], sems.at[0, tile]),
        pltpu.make_async_copy(virt.at[source, :], cols_virt.at[target, :], sems.at[1, tile]),
    )


def over_groups(count, begin, later):
    triple = (lax.rem(count, 2) == 1) & (count >= 3)
    begun = jnp.where(triple, 3, 2)

    @pl.when(triple)
    def _():
        begin(0, 3)

    @pl.when((count > 0) & jnp.logical_not(triple))
    def _():
        begin(0, 2)

    def one_pair(g, carry):
        later(begun + 2 * g, 2)
        return carry

    lax.fori_loop(0, lax.div(loaded_tiles(count) - begun, 2), one_pair, 0)


def tile_range(first, size):
    if isinstance(first, int):
        return pl.ds(first * BLK, size * BLK)
    return pl.ds(pl.multiple_of(first * BLK, BLK), size * BLK)


def polar_part(columns, scaled, cols_occ, cols_virt):
    green_occ = lax.dot_general(
        cols_occ[columns, :], scaled[0][...], NT_DIMS, preferred_element_type=jnp.float32
    )
    green_virt = lax.dot_general(
        cols_virt[columns, :], scaled[1][...], NT_DIMS, preferred_element_type=jnp.float32
    )
    return (green_occ * green_virt).astype(jnp.bfloat16)


def over_tiles(count, scale, copies, scaled, cols_occ, cols_virt, open_group):
    starts = starts_of(scaled)

    def one_group(first, size, begins):
        for tile in range(size):
            for copy in copies(first + tile):
                copy.wait()
        take = open_group(first, size)
        if begins:
            scale(0, False)
        for i, part in enumerate(scaled):
            if begins and i + 1 < len(scaled):
                scale(i + 1, True)
            value = polar_part(tile_range(first, size), part, cols_occ, cols_virt)
            take(i, pl.ds(starts[i], starts[i + 1] - starts[i]), value)

    over_groups(
        count,
        lambda first, size: one_group(first, size, True),
        lambda first, size: one_group(first, size, False),
    )


def start_tiles(copies, count):
    def one_tile(tile, carry):
        for copy in copies(tile):
            copy.start()
        return carry

    lax.fori_loop(0, loaded_tiles(count), one_tile, 0)


def wait_tiles(copies, count):
    def one_tile(tile, carry):
        for copy in copies(tile):
            copy.wait()
        return carry

    lax.fori_loop(0, loaded_tiles(count), one_tile, 0)


def own_kernel(
    plan, table, times, gaps_occ, gaps_virt, occ, virt, polar,
    row_occ, row_virt, scaled, cols_occ, cols_virt, kept, row_sems, tile_sems, save_sems,
):
    which = plan.panels - 1
    slot = lax.div(lax.axis_index("ta"), jnp.int32(lax.axis_size("ta") // plan.blocks))
    own = table[plan.order + slot]
    count = table[which]
    place = pl.ds(pl.multiple_of(own * BLK, BLK), BLK)
    row_copies = (
        pltpu.make_async_copy(occ.at[place, :], row_occ, row_sems.at[0]),
        pltpu.make_async_copy(virt.at[place, :], row_virt, row_sems.at[1]),
    )
    copies = lambda tile: tile_copies(
        plan, table, which, tile, occ, virt, cols_occ, cols_virt, tile_sems
    )
    for copy in row_copies:
        copy.start()
    start_tiles(copies, count)
    for copy in row_copies:
        copy.wait()

    def scale(i, unrolled):
        scale_part(
            starts_of(scaled)[i] // BLK, times, gaps_occ, gaps_virt, row_occ, row_virt,
            scaled[i], unrolled,
        )

    starts = starts_of(scaled)

    def saved(first, size, i):
        part = (tile_range(first, size), pl.ds(starts[i], starts[i + 1] - starts[i]))
        return pltpu.make_async_copy(kept.at[part], polar.at[part], save_sems.at[first, i])

    def open_group(first, size):
        def take(i, part, value):
            kept[tile_range(first, size), part] = value
            saved(first, size, i).start()

        return take

    def finish(first, size):
        for i in range(len(scaled)):
            saved(first, size, i).wait()

    over_tiles(count, scale, copies, scaled, cols_occ, cols_virt, open_group)
    over_groups(count, finish, finish)


def rest_kernel(
    plan, table, times, cosine, gaps_occ, gaps_virt, other_rows, occ, virt, polar, probes,
    out, scaled, cols_occ, cols_virt, kept, fresh, terms,
    probe_two, probe_three, tile_sems, kept_sems,
):
    panels = plan.panels
    here = lax.axis_index("pa")
    rows = terms.shape[2]
    virt_count = virt.shape[1]

    def kept_copies(tile):
        place = tile_range(tile, 1)
        return (
            pltpu.make_async_copy(polar.at[place, :], kept.at[place, :], kept_sems.at[tile]),
        )

    def load_probes(which, first, size):
        held = probe_two if size == 2 else probe_three
        count = table[which]
        for tile in range(size):
            at = jnp.minimum(first + tile, jnp.maximum(count - 1, 0))
            value = probes[here * plan.blocks + table[plan.cols + which * plan.tiles + at]]
            held[:, tile * BLK : (tile + 1) * BLK] = jnp.where(
                first + tile < count, value, jnp.zeros_like(value)
            )
        return held

    terms[...] = jnp.zeros_like(terms)

    def apply(which, count, polars):
        def one_group(first, size):
            held = load_probes(which, first, size)
            terms[which] += jnp.dot(
                held[...], polars[tile_range(first, size), :], preferred_element_type=jnp.float32
            )

        over_groups(count, one_group, one_group)

    def one_other(which, carry):
        count = table[which]
        place = pl.ds(pl.multiple_of(which * BLK, BLK), BLK)
        row_virt = other_rows.at[place, pl.ds(0, virt_count)]
        row_occ = other_rows.at[place, pl.ds(virt_count, occ.shape[1])]
        copies = lambda tile: tile_copies(
            plan, table, which, tile, occ, virt, cols_occ, cols_virt, tile_sems
        )
        start_tiles(copies, count)

        @pl.when(which == 0)
        def _():
            start_tiles(kept_copies, table[panels - 1])

        def scale(i, unrolled):
            scale_part(
                starts_of(scaled)[i] // BLK, times, gaps_occ, gaps_virt, row_occ, row_virt,
                scaled[i], unrolled,
            )

        def open_group(first, size):
            def take(i, part, value):
                fresh[tile_range(first, size), part] = value

            return take

        over_tiles(count, scale, copies, scaled, cols_occ, cols_virt, open_group)
        apply(which, count, fresh)
        return carry

    lax.fori_loop(0, panels - 1, one_other, 0)
    wait_tiles(kept_copies, table[panels - 1])
    apply(panels - 1, table[panels - 1], kept)

    for which in range(panels):
        dest = lax.rem(here + which + 1, panels)

        def some_freqs(g, carry):
            totals = [jnp.zeros((NVEC, BLK), jnp.float32)] * FREQS
            for t in range(rows // BLK):
                value = terms[which, :, t * BLK : (t + 1) * BLK]
                for j in range(FREQS):
                    totals[j] += cosine[g * FREQS + j, t] * value
            for j in range(FREQS):
                out[(g * FREQS + j) * panels + dest] = totals[j]
            return carry

        lax.fori_loop(0, out.shape[0] // (panels * FREQS), some_freqs, 0)


def sum_kernel(plan, group, table, parts, out):
    panels, blocks = plan.panels, plan.blocks
    here = lax.axis_index("pa")
    for slot in range(blocks):
        total = jnp.zeros((NVEC, BLK), jnp.float32)
        for offset in range(1, panels):
            panel = lax.rem(here + offset, panels)
            for member in range(group):
                total += parts[(slot * group + member) * panels + panel]
        out[0, :, slot * BLK : (slot + 1) * BLK] = total
    for slot in range(blocks):
        total = parts[slot * group * panels + here]
        for member in range(1, group):
            total += parts[(slot * group + member) * panels + here]
        place = pl.ds(pl.multiple_of(table[plan.order + slot] * BLK, BLK), BLK)
        out[0, :, place] += total


def shards(
    occupied_orbitals, virtual_orbitals, occupied_gaps, virtual_gaps, tile_columns, probe_vectors
):
    count_ta = lax.axis_size("ta")
    panels = lax.axis_size("pa")
    panel_rows, occ_count = occupied_orbitals.shape
    virt_count = virtual_orbitals.shape[1]
    slice_width = probe_vectors.shape[1]
    tiles = tile_columns.shape[1]
    blocks = panel_rows // BLK
    group = count_ta // blocks
    local_times = NT // group
    rows = local_times * BLK
    if local_times % 8:
        parts_rows = (rows,)
    else:
        parts_rows = tuple(rows * part // 32 for part in (4, 8, 8, 12))
    plan = Plan(panels, tiles, blocks)
    width = min(slice_width, BLK)

    sent = pl.pallas_call(
        functools.partial(pack_kernel, group),
        in_specs=[ANY, ANY],
        out_specs=ANY,
        out_shape=jax.ShapeDtypeStruct((BLK, virt_count + occ_count), jnp.bfloat16),
        scratch_shapes=[pltpu.SemaphoreType.DMA((2,))],
        compiler_params=SMALL,
        name="pack",
    )(occupied_orbitals, virtual_orbitals)
    table, spread = pl.pallas_call(
        functools.partial(plan_kernel, plan, group),
        in_specs=[ANY, ANY, ANY],
        out_specs=(SMEM, VMEM),
        out_shape=(
            jax.ShapeDtypeStruct((plan.size,), jnp.int32),
            jax.ShapeDtypeStruct((count_ta, slice_width // width, NVEC, width), jnp.bfloat16),
        ),
        scratch_shapes=[
            pltpu.SMEM(tile_columns.shape, jnp.int32),
            pltpu.VMEM(probe_vectors.shape, jnp.bfloat16),
            pltpu.SMEM((2, blocks), jnp.int32),
            pltpu.SMEM((2, max(tiles, tiles * (panels - 1)) + 2), jnp.int32),
            pltpu.SMEM((2, blocks), jnp.int32),
            pltpu.SemaphoreType.DMA((2,)),
        ],
        compiler_params=SMALL,
        name="plan",
    )(tile_columns, probe_vectors, sent)

    others = [
        lax.ppermute(sent, "pa", [(q, (q - offset) % panels) for q in range(panels)])
        for offset in range(1, panels)
    ]
    other_rows = others[0] if panels == 2 else jnp.concatenate(others, axis=0)

    probes = lax.all_to_all(spread, "ta", 0, 0, tiled=True)
    if width < BLK:
        probes = probes.reshape(-1, BLK // width, NVEC, width).transpose(0, 2, 1, 3)
    probes = probes.reshape(-1, NVEC, BLK)

    times, cosine = quadrature_grids(NT, count_ta)
    if group > 1:
        first_time = (lax.axis_index("ta") % group) * local_times
        times = lax.dynamic_slice_in_dim(times, first_time, local_times, 0)
        cosine = lax.dynamic_slice_in_dim(cosine, first_time, local_times, 1)

    held_tiles = max(tiles, 2) * BLK
    scratch = [
        [
            (
                pltpu.VMEM((part, occ_count), jnp.bfloat16),
                pltpu.VMEM((part, virt_count), jnp.bfloat16),
            )
            for part in parts_rows
        ],
        pltpu.VMEM((held_tiles, occ_count), jnp.bfloat16),
        pltpu.VMEM((held_tiles, virt_count), jnp.bfloat16),
        pltpu.VMEM((held_tiles, rows), jnp.bfloat16),
    ]
    row_scratch = [
        pltpu.VMEM((BLK, occ_count), jnp.bfloat16),
        pltpu.VMEM((BLK, virt_count), jnp.bfloat16),
    ]
    tile_sems = pltpu.SemaphoreType.DMA((2, max(tiles, 2)))
    cost = pl.CostEstimate(
        flops=tiles * BLK * rows * (occ_count + virt_count), bytes_accessed=2**23, transcendentals=0
    )
    polar = pl.pallas_call(
        functools.partial(own_kernel, plan),
        in_specs=[SMEM, SMEM, VMEM, VMEM, ANY, ANY],
        out_specs=ANY,
        out_shape=jax.ShapeDtypeStruct((held_tiles, rows), jnp.bfloat16),
        scratch_shapes=row_scratch
        + scratch
        + [
            pltpu.SemaphoreType.DMA((2,)),
            tile_sems,
            pltpu.SemaphoreType.DMA((max(tiles, 2), len(parts_rows))),
        ],
        compiler_params=LARGE,
        cost_estimate=cost,
        name="own_tiles",
    )(table, times, occupied_gaps, virtual_gaps, occupied_orbitals, virtual_orbitals)

    partial_response = pl.pallas_call(
        functools.partial(rest_kernel, plan),
        in_specs=[SMEM, SMEM, SMEM, VMEM, VMEM, VMEM, ANY, ANY, ANY, VMEM],
        out_specs=VMEM,
        out_shape=jax.ShapeDtypeStruct((count_ta * panels, NVEC, BLK), jnp.float32),
        scratch_shapes=scratch
        + [
            pltpu.VMEM((held_tiles, rows), jnp.bfloat16),
            pltpu.VMEM((panels, NVEC, rows), jnp.float32),
            pltpu.VMEM((NVEC, 2 * BLK), jnp.bfloat16),
            pltpu.VMEM((NVEC, 3 * BLK), jnp.bfloat16),
        ]
        + [tile_sems, pltpu.SemaphoreType.DMA((max(tiles, 2),))],
        compiler_params=LARGE,
        cost_estimate=cost,
        name="other_tiles",
    )(
        table, times, cosine, occupied_gaps, virtual_gaps, other_rows,
        occupied_orbitals, virtual_orbitals, polar, probes,
    )

    parts = lax.all_to_all(partial_response, ("ta", "pa"), 0, 0, tiled=True)
    return pl.pallas_call(
        functools.partial(sum_kernel, plan, group),
        in_specs=[SMEM, VMEM],
        out_specs=VMEM,
        out_shape=jax.ShapeDtypeStruct((1, NVEC, panel_rows), jnp.float32),
        compiler_params=SMALL,
        name="sum_parts",
    )(table, parts)


def solution(mesh):
    placed = (P("pa", None), P("pa", None), P(), P(), P(), P(None, "ta"))
    return jax.shard_map(
        shards, mesh=mesh, in_specs=placed, out_specs=P("ta", None, "pa"), check_vma=False
    )
```

profile of v0, /device:TPU:1, one launch (start us, length us, event | category | flops | bytes accessed | tf_op | source)
XLA Modules:
  0.0 67.1 jit_solution(15515839292430674846)
XLA Ops:
  0.0 0.0 copy-start.3
  0.0 0.0 copy-start
  0.0 0.0 copy-start.1
  0.0 0.0 copy-start.2
  0.0 1.1 %pack.1.after = bf16[128,2048]{1,0:T(8,128)(2,1)S(1)} custom-call(bf16[2048,512]{1,0:T(8,128)(2,1)} %occ.5, bf16[2048,1536]{1,0:T(8,128)(2,1)} %virt.5), custom_call_target="tpu_custom_call" | custom-call | tf_op jit(solution)/shard_map/pack/pallas_call | solution.py:429
  1.1 2.1 %collective-permute-start = (bf16[128,2048]{1,0:T(8,128)(2,1)S(1)}, bf16[128,2048]{1,0:T(8,128)(2,1)S(1)}, u32[]{:S(2)}, u32[]{:S(2)}) collective-permute-start(bf16[128,2048]{1,0:T(8,128)(2,1)S(1)} %pack.1.after), channel_id=1, source_target_pairs={{0,1},{1,0},{2,3},{3,2},{4,5},{5,4},{6,7},{7,6},{8,9},{9,8},{10,11... | collective-permute-start | bytes 1572872 | tf_op jit(solution)/shard_map/ppermute | solution.py:459
  3.2 0.0 copy-done.3
  3.2 0.1 copy.7.tiles_hbm
  3.3 0.0 copy-done
  3.3 2.8 %plan.1 = (s32[34]{0:T(128)S(1)}, bf16[16,2,32,128]{3,2,1,0:T(8,128)(2,1)}) custom-call(s32[32,8]{1,0:T(8,128)S(1)} %copy.7.tiles_hbm, bf16[32,256]{1,0:T(8,128)(2,1)S(1)} %copy-done, bf16[128,2048]{1,0:T(8,128)(2,1)S(1)} %pack.1.after), custom_call_target="tpu_custom_call" | custom-call | tf_op jit(solution)/shard_map/plan/pallas_call | solution.py:438
  6.1 6.8 %all-to-all-start = ((bf16[16,2,32,128]{3,2,1,0:T(8,128)(2,1)}), bf16[16,2,32,128]{3,2,1,0:T(8,128)(2,1)S(1)}, u32[]{:S(2)}, u32[]{:S(2)}) async-start(bf16[16,2,32,128]{3,2,1,0:T(8,128)(2,1)} %get-tuple-element.8), calls=%async_computation | async-start | bytes 524288 | tf_op jit(solution)/shard_map/all_to_all | solution.py:464
  12.9 0.0 copy-done.1
  12.9 0.0 copy-done.2
  12.9 13.1 %own_tiles.1.polar = bf16[1024,4096]{1,0:T(8,128)(2,1)} custom-call(s32[34]{0:T(128)S(1)} %get-tuple-element.7.table, f32[32]{0:T(128)S(1)} %get-tuple-element.9.times, f32[512]{0:T(512)S(1)} %copy-done.2, f32[1536]{0:T(1024)S(1)} %copy-done.1, bf16[2048,512]{1,0:T(8,128)(2,1)} %occ.5, bf16[2048,1536]{1,0:T(8,128)(2,1)} %virt.5), custom_call_target="tpu_custom_call" | custom-call | flops 8589934592 | bytes 8388608 | tf_op jit(solution)/shard_map/own_tiles/pallas_call | solution.py:496
  26.0 0.1 cosine_multiply_fusion.cosine
  26.2 0.0 all-to-all-done
  26.2 0.0 collective-permute-done.other_rows
  26.2 12.8 %other_tiles.1 = f32[32,32,128]{2,1,0:T(8,128)S(1)} custom-call(s32[34]{0:T(128)S(1)} %get-tuple-element.7.table, f32[32]{0:T(128)S(1)} %get-tuple-element.9.times, f32[16,32]{1,0:T(8,128)S(1)} %cosine_multiply_fusion.cosine, f32[512]{0:T(512)S(1)} %copy-done.2, f32[1536]{0:T(1024)S(1)} %copy-done.1, bf16[128,2048]{1,0:T(8,128)(2,1)S(1)} %collective-permute-done.other_rows, ...), custom_call_target="tpu_custom_call" | custom-call | flops 8589934592 | bytes 8388608 | tf_op jit(solution)/shard_map/other_tiles/pallas_call | solution.py:513
  39.0 26.7 %all_to_all.10.parts = f32[32,32,128]{2,1,0:T(8,128)S(1)} all-to-all(f32[32,32,128]{2,1,0:T(8,128)S(1)} %other_tiles.1), channel_id=1, replica_groups=mesh['ta'=16,'pa'=2] {'ta','pa'}, dimensions={0} | all-to-all | bytes 1048576 | tf_op jit(solution)/shard_map/all_to_all | solution.py:534
  65.7 1.3 %sum_parts.1 = f32[1,32,2048]{2,1,0:T(8,128)} custom-call(s32[34]{0:T(128)S(1)} %get-tuple-element.7.table, f32[32,32,128]{2,1,0:T(8,128)S(1)} %all_to_all.10.parts), custom_call_target="tpu_custom_call" | custom-call | tf_op jit(solution)/shard_map/sum_parts/pallas_call | solution.py:535
  (2 shorter events, 0.0 us)
Async XLA Ops:
  0.0 3.2 %copy-start.3 = (s32[32,8]{0,1:T(8,128)S(1)}, s32[32,8]{0,1:T(8,128)}, u32[]{:S(2)}) copy-start(s32[32,8]{0,1:T(8,128)} %param.10) | copy-start | bytes 3076
  0.0 3.3 %copy-start = (bf16[32,256]{1,0:T(8,128)(2,1)S(1)}, bf16[32,256]{1,0:T(8,128)(2,1)}, u32[]{:S(2)}) copy-start(bf16[32,256]{1,0:T(8,128)(2,1)} %probe_hbm.1) | copy-start | bytes 49156
  0.0 12.9 %copy-start.1 = (f32[1536]{0:T(1024)S(1)}, f32[1536]{0:T(1024)}, u32[]{:S(2)}) copy-start(f32[1536]{0:T(1024)} %gaps_virt.3) | copy-start | bytes 18436
  0.0 12.9 %copy-start.2 = (f32[512]{0:T(512)S(1)}, f32[512]{0:T(512)}, u32[]{:S(2)}) copy-start(f32[512]{0:T(512)} %gaps_occ.3) | copy-start | bytes 6148
  1.1 25.1 %collective-permute-start = (bf16[128,2048]{1,0:T(8,128)(2,1)S(1)}, bf16[128,2048]{1,0:T(8,128)(2,1)S(1)}, u32[]{:S(2)}, u32[]{:S(2)}) collective-permute-start(bf16[128,2048]{1,0:T(8,128)(2,1)S(1)} %pack.1.after), channel_id=1, source_target_pairs={{0,1},{1,0},{2,3},{3,2},{4,5},{5,4},{6,7},{7,6},{8,9},{9,8},{10,11... | collective-permute-start | bytes 1572872 | tf_op jit(solution)/shard_map/ppermute | solution.py:459
  6.1 20.1 %all-to-all-start = ((bf16[16,2,32,128]{3,2,1,0:T(8,128)(2,1)}), bf16[16,2,32,128]{3,2,1,0:T(8,128)(2,1)S(1)}, u32[]{:S(2)}, u32[]{:S(2)}) async-start(bf16[16,2,32,128]{3,2,1,0:T(8,128)(2,1)} %get-tuple-element.8), calls=%async_computation | async-start | bytes 524288 | tf_op jit(solution)/shard_map/all_to_all | solution.py:464
where the time goes:
time: 67 us; the launch traced here: 67.1 us
  Pallas kernels  31.1 us (46%)
  blocking collectives  26.7 us (40%)
  starting transfers between devices  8.92 us (13%)
    all_to_all x1, blocking collectives, shards(): parts = lax.all_to_all(partial_response, ('ta', 'pa'), 0, 0, tiled=True)  26.7 us
    pallas_call x1, Pallas kernels, shards(): pl.pallas_call(functools.partial(own_kernel, plan), in_specs=[SMEM, SMEM,...  13.1 us
    pallas_call x1, Pallas kernels, shards(): pl.pallas_call(functools.partial(rest_kernel, plan), in_specs=[SMEM, SMEM...  12.8 us
    all_to_all x1, starting transfers between devices, shards(): probes = lax.all_to_all(spread, 'ta', 0, 0, tiled=True)  6.78 us
    pallas_call x1, Pallas kernels, shards(): pl.pallas_call(functools.partial(plan_kernel, plan, group), in_specs=[ANY...  2.76 us
    ppermute x1, starting transfers between devices, shards(): lax.ppermute(sent, 'pa', [(q, (q - offset) % panels) for q in range(panel...  2.13 us
    pallas_call x1, Pallas kernels, shards(): pl.pallas_call(functools.partial(sum_kernel, plan, group), in_specs=[SMEM...  1.35 us
  transfers between devices with their start and end apart: 2, of which 0 were waited for; matrix products, arithmetic and copies ran while one was open for 0% of the time, Pallas kernels for 24%

commit v1 on v0

--- a/solution.py
+++ b/solution.py
@@ -214,12 +214,12 @@
     starts = starts_of(scaled)
 
     def one_group(first, size, begins):
+        if begins:
+            scale(0, False)
         for tile in range(size):
             for copy in copies(first + tile):
                 copy.wait()
         take = open_group(first, size)
-        if begins:
-            scale(0, False)
         for i, part in enumerate(scaled):
             if begins and i + 1 < len(scaled):
                 scale(i + 1, True)

time: 67 us -> 64.9 us (0.969); the launches traced: 67.1 us -> 64.2 us
  blocking collectives: 26.7 us -> 24.5 us
  Pallas kernels: 31.1 us -> 30.4 us
    pallas_call x1, Pallas kernels: 13.1 us -> 10.4 us  [shards(): pl.pallas_call(functools.partial(own_kernel, plan), in_specs=[SMEM, SMEM,...]
    all_to_all x1, blocking collectives: 26.7 us -> 24.5 us  [shards(): parts = lax.all_to_all(partial_response, ('ta', 'pa'), 0, 0, tiled=True)]
    pallas_call x1, Pallas kernels: 12.8 us -> 14.8 us  [shards(): pl.pallas_call(functools.partial(rest_kernel, plan), in_specs=[SMEM, SMEM...]
  transfers between devices with their start and end apart: 2 -> 2, of which waited for: 0 -> 0; matrix products, arithmetic and copies ran while one was open for 0% -> 0% of each run, Pallas kernels for 24% -> 20%
where the time goes in v1:
time: 64.9 us; the launch traced here: 64.2 us
  Pallas kernels  30.4 us (47%)
  blocking collectives  24.5 us (38%)
  starting transfers between devices  8.92 us (14%)
    all_to_all x1, blocking collectives, shards(): parts = lax.all_to_all(partial_response, ('ta', 'pa'), 0, 0, tiled=True)  24.5 us
    pallas_call x1, Pallas kernels, shards(): pl.pallas_call(functools.partial(rest_kernel, plan), in_specs=[SMEM, SMEM...  14.8 us
    pallas_call x1, Pallas kernels, shards(): pl.pallas_call(functools.partial(own_kernel, plan), in_specs=[SMEM, SMEM,...  10.4 us
    all_to_all x1, starting transfers between devices, shards(): probes = lax.all_to_all(spread, 'ta', 0, 0, tiled=True)  6.78 us
    pallas_call x1, Pallas kernels, shards(): pl.pallas_call(functools.partial(plan_kernel, plan, group), in_specs=[ANY...  2.76 us
    ppermute x1, starting transfers between devices, shards(): lax.ppermute(sent, 'pa', [(q, (q - offset) % panels) for q in range(panel...  2.13 us
    pallas_call x1, Pallas kernels, shards(): pl.pallas_call(functools.partial(sum_kernel, plan, group), in_specs=[SMEM...  1.35 us
  transfers between devices with their start and end apart: 2, of which 0 were waited for; matrix products, arithmetic and copies ran while one was open for 0% of the time, Pallas kernels for 20%

profile of v1, /device:TPU:1, one launch (start us, length us, event | category | flops | bytes accessed | tf_op | source)
XLA Modules:
  0.0 64.2 jit_solution(7119670549279987838)
XLA Ops:
  0.0 0.0 copy-start.3
  0.0 0.0 copy-start
  0.0 0.0 copy-start.1
  0.0 0.0 copy-start.2
  0.0 1.1 %pack.1.after = bf16[128,2048]{1,0:T(8,128)(2,1)S(1)} custom-call(bf16[2048,512]{1,0:T(8,128)(2,1)} %occ.5, bf16[2048,1536]{1,0:T(8,128)(2,1)} %virt.5), custom_call_target="tpu_custom_call" | custom-call | tf_op jit(solution)/shard_map/pack/pallas_call | solution.py:429
  1.1 2.1 %collective-permute-start = (bf16[128,2048]{1,0:T(8,128)(2,1)S(1)}, bf16[128,2048]{1,0:T(8,128)(2,1)S(1)}, u32[]{:S(2)}, u32[]{:S(2)}) collective-permute-start(bf16[128,2048]{1,0:T(8,128)(2,1)S(1)} %pack.1.after), channel_id=1, source_target_pairs={{0,1},{1,0},{2,3},{3,2},{4,5},{5,4},{6,7},{7,6},{8,9},{9,8},{10,11... | collective-permute-start | bytes 1572872 | tf_op jit(solution)/shard_map/ppermute | solution.py:459
  3.2 0.0 copy-done.3
  3.2 0.1 copy.7.tiles_hbm
  3.3 0.0 copy-done
  3.3 2.8 %plan.1 = (s32[34]{0:T(128)S(1)}, bf16[16,2,32,128]{3,2,1,0:T(8,128)(2,1)}) custom-call(s32[32,8]{1,0:T(8,128)S(1)} %copy.7.tiles_hbm, bf16[32,256]{1,0:T(8,128)(2,1)S(1)} %copy-done, bf16[128,2048]{1,0:T(8,128)(2,1)S(1)} %pack.1.after), custom_call_target="tpu_custom_call" | custom-call | tf_op jit(solution)/shard_map/plan/pallas_call | solution.py:438
  6.1 6.8 %all-to-all-start = ((bf16[16,2,32,128]{3,2,1,0:T(8,128)(2,1)}), bf16[16,2,32,128]{3,2,1,0:T(8,128)(2,1)S(1)}, u32[]{:S(2)}, u32[]{:S(2)}) async-start(bf16[16,2,32,128]{3,2,1,0:T(8,128)(2,1)} %get-tuple-element.8), calls=%async_computation | async-start | bytes 524288 | tf_op jit(solution)/shard_map/all_to_all | solution.py:464
  12.9 0.0 copy-done.1
  12.9 0.0 copy-done.2
  12.9 10.4 %own_tiles.1.polar = bf16[1024,4096]{1,0:T(8,128)(2,1)} custom-call(s32[34]{0:T(128)S(1)} %get-tuple-element.7.table, f32[32]{0:T(128)S(1)} %get-tuple-element.9.times, f32[512]{0:T(512)S(1)} %copy-done.2, f32[1536]{0:T(1024)S(1)} %copy-done.1, bf16[2048,512]{1,0:T(8,128)(2,1)} %occ.5, bf16[2048,1536]{1,0:T(8,128)(2,1)} %virt.5), custom_call_target="tpu_custom_call" | custom-call | flops 8589934592 | bytes 8388608 | tf_op jit(solution)/shard_map/own_tiles/pallas_call | solution.py:496
  23.3 0.1 cosine_multiply_fusion.cosine
  23.4 0.0 all-to-all-done
  23.5 0.0 collective-permute-done.other_rows
  23.5 14.8 %other_tiles.1 = f32[32,32,128]{2,1,0:T(8,128)S(1)} custom-call(s32[34]{0:T(128)S(1)} %get-tuple-element.7.table, f32[32]{0:T(128)S(1)} %get-tuple-element.9.times, f32[16,32]{1,0:T(8,128)S(1)} %cosine_multiply_fusion.cosine, f32[512]{0:T(512)S(1)} %copy-done.2, f32[1536]{0:T(1024)S(1)} %copy-done.1, bf16[128,2048]{1,0:T(8,128)(2,1)S(1)} %collective-permute-done.other_rows, ...), custom_call_target="tpu_custom_call" | custom-call | flops 8589934592 | bytes 8388608 | tf_op jit(solution)/shard_map/other_tiles/pallas_call | solution.py:513
  38.3 24.5 %all_to_all.10.parts = f32[32,32,128]{2,1,0:T(8,128)S(1)} all-to-all(f32[32,32,128]{2,1,0:T(8,128)S(1)} %other_tiles.1), channel_id=1, replica_groups=mesh['ta'=16,'pa'=2] {'ta','pa'}, dimensions={0} | all-to-all | bytes 1048576 | tf_op jit(solution)/shard_map/all_to_all | solution.py:534
  62.8 1.3 %sum_parts.1 = f32[1,32,2048]{2,1,0:T(8,128)} custom-call(s32[34]{0:T(128)S(1)} %get-tuple-element.7.table, f32[32,32,128]{2,1,0:T(8,128)S(1)} %all_to_all.10.parts), custom_call_target="tpu_custom_call" | custom-call | tf_op jit(solution)/shard_map/sum_parts/pallas_call | solution.py:535
  (2 shorter events, 0.0 us)
Async XLA Ops:
  0.0 3.2 %copy-start.3 = (s32[32,8]{0,1:T(8,128)S(1)}, s32[32,8]{0,1:T(8,128)}, u32[]{:S(2)}) copy-start(s32[32,8]{0,1:T(8,128)} %param.10) | copy-start | bytes 3076
  0.0 3.3 %copy-start = (bf16[32,256]{1,0:T(8,128)(2,1)S(1)}, bf16[32,256]{1,0:T(8,128)(2,1)}, u32[]{:S(2)}) copy-start(bf16[32,256]{1,0:T(8,128)(2,1)} %probe_hbm.1) | copy-start | bytes 49156
  0.0 12.9 %copy-start.1 = (f32[1536]{0:T(1024)S(1)}, f32[1536]{0:T(1024)}, u32[]{:S(2)}) copy-start(f32[1536]{0:T(1024)} %gaps_virt.3) | copy-start | bytes 18436
  0.0 12.9 %copy-start.2 = (f32[512]{0:T(512)S(1)}, f32[512]{0:T(512)}, u32[]{:S(2)}) copy-start(f32[512]{0:T(512)} %gaps_occ.3) | copy-start | bytes 6148
  1.1 22.3 %collective-permute-start = (bf16[128,2048]{1,0:T(8,128)(2,1)S(1)}, bf16[128,2048]{1,0:T(8,128)(2,1)S(1)}, u32[]{:S(2)}, u32[]{:S(2)}) collective-permute-start(bf16[128,2048]{1,0:T(8,128)(2,1)S(1)} %pack.1.after), channel_id=1, source_target_pairs={{0,1},{1,0},{2,3},{3,2},{4,5},{5,4},{6,7},{7,6},{8,9},{9,8},{10,11... | collective-permute-start | bytes 1572872 | tf_op jit(solution)/shard_map/ppermute | solution.py:459
  6.1 17.4 %all-to-all-start = ((bf16[16,2,32,128]{3,2,1,0:T(8,128)(2,1)}), bf16[16,2,32,128]{3,2,1,0:T(8,128)(2,1)S(1)}, u32[]{:S(2)}, u32[]{:S(2)}) async-start(bf16[16,2,32,128]{3,2,1,0:T(8,128)(2,1)} %get-tuple-element.8), calls=%async_computation | async-start | bytes 524288 | tf_op jit(solution)/shard_map/all_to_all | solution.py:464

commit v2 on v1

--- a/solution.py
+++ b/solution.py
@@ -40,7 +40,8 @@
         self.blocks = blocks
         self.cols = panels
         self.order = panels + panels * tiles
-        self.size = self.order + blocks
+        self.slots = self.order + blocks
+        self.size = self.slots + blocks
 
 
 def pack_kernel(group, occ, virt, sent, sems):
@@ -116,6 +117,7 @@
     lax.fori_loop(0, blocks, one_place, 0)
     for rank in range(blocks):
         out[plan.order + ranked[1, rank]] = ranked[0, rank]
+        out[plan.slots + ranked[0, rank]] = ranked[1, rank]
 
     for which in range(panels):
         if which < panels - 1:
@@ -388,22 +390,31 @@
         lax.fori_loop(0, out.shape[0] // (panels * FREQS), some_freqs, 0)
 
 
-def sum_kernel(plan, group, table, parts, out):
+def sum_kernel(plan, group, table, parts, out, total, sems):
     panels, blocks = plan.panels, plan.blocks
     here = lax.axis_index("pa")
-    for slot in range(blocks):
-        total = jnp.zeros((NVEC, BLK), jnp.float32)
+    piece = blocks // sems.shape[0]
+    copies = []
+    for block in range(blocks):
+        own = table[plan.slots + block] * (group * panels) + here
+        value = parts[own]
+        for member in range(1, group):
+            value += parts[own + member * panels]
         for offset in range(1, panels):
             panel = lax.rem(here + offset, panels)
             for member in range(group):
-                total += parts[(slot * group + member) * panels + panel]
-        out[0, :, slot * BLK : (slot + 1) * BLK] = total
-    for slot in range(blocks):
-        total = parts[slot * group * panels + here]
-        for member in range(1, group):
-            total += parts[(slot * group + member) * panels + here]
-        place = pl.ds(pl.multiple_of(table[plan.order + slot] * BLK, BLK), BLK)
-        out[0, :, place] += total
+                value += parts[(block * group + member) * panels + panel]
+        total[0, :, block * BLK : (block + 1) * BLK] = value
+        if (block + 1) % piece == 0:
+            columns = pl.ds((block + 1 - piece) * BLK, piece * BLK)
+            copies.append(
+                pltpu.make_async_copy(
+                    total.at[:, :, columns], out.at[:, :, columns], sems.at[block // piece]
+                )
+            )
+            copies[-1].start()
+    for copy in copies:
+        copy.wait()
 
 
 def shards(
@@ -535,8 +546,12 @@
     return pl.pallas_call(
         functools.partial(sum_kernel, plan, group),
         in_specs=[SMEM, VMEM],
-        out_specs=VMEM,
+        out_specs=ANY,
         out_shape=jax.ShapeDtypeStruct((1, NVEC, panel_rows), jnp.float32),
+        scratch_shapes=[
+            pltpu.VMEM((1, NVEC, panel_rows), jnp.float32),
+            pltpu.SemaphoreType.DMA((4,)),
+        ],
         compiler_params=SMALL,
         name="sum_parts",
     )(table, parts)

time: 64.9 us -> 65 us (level)
  Pallas kernels: 30.4 us -> 32.7 us
  blocking collectives: 24.5 us -> 22.2 us
    pallas_call x1, Pallas kernels: 10.4 us -> 15 us  [shards(): pl.pallas_call(functools.partial(own_kernel, plan), in_specs=[SMEM, SMEM,...]
    all_to_all x1, blocking collectives: 24.5 us -> 22.2 us  [shards(): parts = lax.all_to_all(partial_response, ('ta', 'pa'), 0, 0, tiled=True)]
    pallas_call x1, Pallas kernels: 14.8 us -> 12.6 us  [shards(): pl.pallas_call(functools.partial(rest_kernel, plan), in_specs=[SMEM, SMEM...]
  transfers between devices with their start and end apart: 2 -> 2, of which waited for: 0 -> 0; matrix products, arithmetic and copies ran while one was open for 0% -> 0% of each run, Pallas kernels for 20% -> 28%
where the time goes in v2:
time: 65 us; the launch traced here: 64.4 us
  Pallas kernels  32.7 us (50%)
  blocking collectives  22.2 us (34%)
  starting transfers between devices  8.92 us (14%)
    all_to_all x1, blocking collectives, shards(): parts = lax.all_to_all(partial_response, ('ta', 'pa'), 0, 0, tiled=True)  22.2 us
    pallas_call x1, Pallas kernels, shards(): pl.pallas_call(functools.partial(own_kernel, plan), in_specs=[SMEM, SMEM,...  15 us
    pallas_call x1, Pallas kernels, shards(): pl.pallas_call(functools.partial(rest_kernel, plan), in_specs=[SMEM, SMEM...  12.6 us
    all_to_all x1, starting transfers between devices, shards(): probes = lax.all_to_all(spread, 'ta', 0, 0, tiled=True)  6.78 us
    pallas_call x1, Pallas kernels, shards(): pl.pallas_call(functools.partial(plan_kernel, plan, group), in_specs=[ANY...  2.77 us
    ppermute x1, starting transfers between devices, shards(): lax.ppermute(sent, 'pa', [(q, (q - offset) % panels) for q in range(panel...  2.13 us
  transfers between devices with their start and end apart: 2, of which 0 were waited for; matrix products, arithmetic and copies ran while one was open for 0% of the time, Pallas kernels for 28%

profile of v2, /device:TPU:1, one launch (start us, length us, event | category | flops | bytes accessed | tf_op | source)
XLA Modules:
  0.0 64.4 jit_solution(3413671470182043290)
XLA Ops:
  0.0 0.0 copy-start.3
  0.0 0.0 copy-start
  0.0 0.0 copy-start.1
  0.0 0.0 copy-start.2
  0.0 1.1 %pack.1.after = bf16[128,2048]{1,0:T(8,128)(2,1)S(1)} custom-call(bf16[2048,512]{1,0:T(8,128)(2,1)} %occ.5, bf16[2048,1536]{1,0:T(8,128)(2,1)} %virt.5), custom_call_target="tpu_custom_call" | custom-call | tf_op jit(solution)/shard_map/pack/pallas_call | solution.py:440
  1.1 2.1 %collective-permute-start = (bf16[128,2048]{1,0:T(8,128)(2,1)S(1)}, bf16[128,2048]{1,0:T(8,128)(2,1)S(1)}, u32[]{:S(2)}, u32[]{:S(2)}) collective-permute-start(bf16[128,2048]{1,0:T(8,128)(2,1)S(1)} %pack.1.after), channel_id=1, source_target_pairs={{0,1},{1,0},{2,3},{3,2},{4,5},{5,4},{6,7},{7,6},{8,9},{9,8},{10,11... | collective-permute-start | bytes 1572872 | tf_op jit(solution)/shard_map/ppermute | solution.py:470
  3.2 0.0 copy-done.3
  3.2 0.1 copy.7.tiles_hbm
  3.3 0.0 copy-done
  3.3 2.8 %plan.1 = (s32[50]{0:T(128)S(1)}, bf16[16,2,32,128]{3,2,1,0:T(8,128)(2,1)}) custom-call(s32[32,8]{1,0:T(8,128)S(1)} %copy.7.tiles_hbm, bf16[32,256]{1,0:T(8,128)(2,1)S(1)} %copy-done, bf16[128,2048]{1,0:T(8,128)(2,1)S(1)} %pack.1.after), custom_call_target="tpu_custom_call" | custom-call | tf_op jit(solution)/shard_map/plan/pallas_call | solution.py:449
  6.1 6.8 %all-to-all-start = ((bf16[16,2,32,128]{3,2,1,0:T(8,128)(2,1)}), bf16[16,2,32,128]{3,2,1,0:T(8,128)(2,1)S(1)}, u32[]{:S(2)}, u32[]{:S(2)}) async-start(bf16[16,2,32,128]{3,2,1,0:T(8,128)(2,1)} %get-tuple-element.8), calls=%async_computation | async-start | bytes 524288 | tf_op jit(solution)/shard_map/all_to_all | solution.py:475
  12.9 0.0 copy-done.1
  12.9 0.0 copy-done.2
  12.9 15.0 %own_tiles.1.polar = bf16[1024,4096]{1,0:T(8,128)(2,1)} custom-call(s32[50]{0:T(128)S(1)} %get-tuple-element.7.table, f32[32]{0:T(128)S(1)} %get-tuple-element.9.times, f32[512]{0:T(512)S(1)} %copy-done.2, f32[1536]{0:T(1024)S(1)} %copy-done.1, bf16[2048,512]{1,0:T(8,128)(2,1)} %occ.5, bf16[2048,1536]{1,0:T(8,128)(2,1)} %virt.5), custom_call_target="tpu_custom_call" | custom-call | flops 8589934592 | bytes 8388608 | tf_op jit(solution)/shard_map/own_tiles/pallas_call | solution.py:507
  27.9 0.1 cosine_multiply_fusion.cosine
  28.0 0.0 all-to-all-done
  28.0 0.0 collective-permute-done.other_rows
  28.0 12.6 %other_tiles.1 = f32[32,32,128]{2,1,0:T(8,128)S(1)} custom-call(s32[50]{0:T(128)S(1)} %get-tuple-element.7.table, f32[32]{0:T(128)S(1)} %get-tuple-element.9.times, f32[16,32]{1,0:T(8,128)S(1)} %cosine_multiply_fusion.cosine, f32[512]{0:T(512)S(1)} %copy-done.2, f32[1536]{0:T(1024)S(1)} %copy-done.1, bf16[128,2048]{1,0:T(8,128)(2,1)S(1)} %collective-permute-done.other_rows, ...), custom_call_target="tpu_custom_call" | custom-call | flops 8589934592 | bytes 8388608 | tf_op jit(solution)/shard_map/other_tiles/pallas_call | solution.py:524
  40.7 22.2 %all_to_all.10.parts = f32[32,32,128]{2,1,0:T(8,128)S(1)} all-to-all(f32[32,32,128]{2,1,0:T(8,128)S(1)} %other_tiles.1), channel_id=1, replica_groups=mesh['ta'=16,'pa'=2] {'ta','pa'}, dimensions={0} | all-to-all | bytes 1048576 | tf_op jit(solution)/shard_map/all_to_all | solution.py:545
  62.9 1.3 %sum_parts.1 = f32[1,32,2048]{2,1,0:T(8,128)} custom-call(s32[50]{0:T(128)S(1)} %get-tuple-element.7.table, f32[32,32,128]{2,1,0:T(8,128)S(1)} %all_to_all.10.parts), custom_call_target="tpu_custom_call" | custom-call | tf_op jit(solution)/shard_map/sum_parts/pallas_call | solution.py:546
  (2 shorter events, 0.0 us)
Async XLA Ops:
  0.0 3.2 %copy-start.3 = (s32[32,8]{0,1:T(8,128)S(1)}, s32[32,8]{0,1:T(8,128)}, u32[]{:S(2)}) copy-start(s32[32,8]{0,1:T(8,128)} %param.10) | copy-start | bytes 3076
  0.0 3.3 %copy-start = (bf16[32,256]{1,0:T(8,128)(2,1)S(1)}, bf16[32,256]{1,0:T(8,128)(2,1)}, u32[]{:S(2)}) copy-start(bf16[32,256]{1,0:T(8,128)(2,1)} %probe_hbm.1) | copy-start | bytes 49156
  0.0 12.9 %copy-start.1 = (f32[1536]{0:T(1024)S(1)}, f32[1536]{0:T(1024)}, u32[]{:S(2)}) copy-start(f32[1536]{0:T(1024)} %gaps_virt.3) | copy-start | bytes 18436
  0.0 12.9 %copy-start.2 = (f32[512]{0:T(512)S(1)}, f32[512]{0:T(512)}, u32[]{:S(2)}) copy-start(f32[512]{0:T(512)} %gaps_occ.3) | copy-start | bytes 6148
  1.1 26.9 %collective-permute-start = (bf16[128,2048]{1,0:T(8,128)(2,1)S(1)}, bf16[128,2048]{1,0:T(8,128)(2,1)S(1)}, u32[]{:S(2)}, u32[]{:S(2)}) collective-permute-start(bf16[128,2048]{1,0:T(8,128)(2,1)S(1)} %pack.1.after), channel_id=1, source_target_pairs={{0,1},{1,0},{2,3},{3,2},{4,5},{5,4},{6,7},{7,6},{8,9},{9,8},{10,11... | collective-permute-start | bytes 1572872 | tf_op jit(solution)/shard_map/ppermute | solution.py:470
  6.1 21.9 %all-to-all-start = ((bf16[16,2,32,128]{3,2,1,0:T(8,128)(2,1)}), bf16[16,2,32,128]{3,2,1,0:T(8,128)(2,1)S(1)}, u32[]{:S(2)}, u32[]{:S(2)}) async-start(bf16[16,2,32,128]{3,2,1,0:T(8,128)(2,1)} %get-tuple-element.8), calls=%async_computation | async-start | bytes 524288 | tf_op jit(solution)/shard_map/all_to_all | solution.py:475
